TPU v7x, 1024 devices: a whole 4x8x16 slice. The times are simulated.
1024 devices in a mesh: row: 128 (over y_hi, x, z), rep: 8 (over y_lo, core).
Axes of the slice: x: 4, y: 8 (y_hi: 2, y_lo: 4; y = y_hi * 4 + y_lo), z: 16, core: 2. Of those that a mesh axis runs over, the one named last changes fastest.
Arguments:
- features: bfloat16 [131072, 256], P(('row', 'rep')), may hold values from -6 to 6
- weight: bfloat16 [256, 256], replicated, may hold values from -0.375 to 0.375
- bias: float32 [256], replicated, may hold values from -3 to 3
- dense_adj: bfloat16 [128, 8, 5, 1024, 128], P('row', 'rep'), may hold values from -0.078125 to 0.078125
- dense_mask: int32 [128, 8, 5, 8, 1], P('row', 'rep'), may hold values 0 or 1
- sparse_adj: bfloat16 [128, 8, 1024, 768], P('row', 'rep'), may hold values from -0.078125 to 0.078125
- sparse_cols: int32 [128, 8, 6], P('row', 'rep'), may hold values from 0 to 7
- sparse_count: int32 [128, 8], P('row', 'rep'), may hold values from 1 to 6, as said below
- cotangent: bfloat16 [131072, 256], P(('row', 'rep')), may hold values from -0.015625 to 0.015625
Outputs:
- activated: bfloat16 [131072, 256], P(('row', 'rep'))
- weight_grad: float32 [256, 256], replicated
- bias_grad: float32 [256], replicated
Inputs may be any that keep to these rules, and one draw needn't show every extreme that they name: `sparse_count`: some device has all 6 slots live.
All inputs are finite; a program needn't handle non-finite values. No bound on the sum of `dense_mask` on one device may be relied on, other than what follows from the above.
Results may differ from a plain program's by a relative error of at most 0.017.
Values may be sent and summed in bfloat16 or wider, within the bound.
No kernel may reach another device: no remote copies, remote signals or barrier semaphores. Data moves between devices by JAX's collectives and lax.ppermute only.
A program may use at most 32 MiB of HBM per device.

v0:
```python
import jax
import jax.numpy as jnp
from jax import lax
from jax.sharding import PartitionSpec as P

BLK = 128


def shifted(value, axis, steps):
    count = lax.axis_size(axis)
    pairs = [(source, (source + steps) % count) for source in range(count)]
    return lax.ppermute(value, axis, pairs)


def on_device(
    features, weight, bias, dense_adj, dense_mask, sparse_adj, sparse_cols, sparse_count, cotangent
):
    dense_tiles = dense_adj[0, 0]
    band_count, panel_rows, piece_rows = dense_tiles.shape
    reach = (band_count - 1) // 2
    feature_width = features.shape[1]
    keep_mask = dense_mask[0, 0][:, :, None, :, None] > 0
    shaped = dense_tiles.reshape(band_count, panel_rows // BLK, BLK, piece_rows // BLK, BLK)
    masked = jnp.where(keep_mask, shaped, jnp.zeros_like(shaped)).reshape(
        band_count, panel_rows, piece_rows
    )
    fetched = {0: features}
    for direction in (1, -1):
        current = features
        for distance in range(1, reach + 1):
            current = shifted(current, "row", direction)
            fetched[-direction * distance] = current
    summed = jnp.zeros((panel_rows, feature_width), jnp.float32)
    for offset in range(band_count):
        summed = summed + jnp.dot(
            masked[offset], fetched[offset - reach], preferred_element_type=jnp.float32
        )
    slot_count = sparse_cols.shape[2]
    my_cols = sparse_cols[0, 0]
    live_slots = jnp.arange(slot_count, dtype=jnp.int32) < sparse_count[0, 0]
    whole_panel = lax.all_gather(features, "rep", axis=0, tiled=True)
    blocks = whole_panel.reshape(panel_rows // BLK, BLK, feature_width)[my_cols]
    blocks = jnp.where(live_slots[:, None, None], blocks, jnp.zeros_like(blocks)).reshape(
        slot_count * BLK, feature_width
    )
    summed = summed + jnp.dot(sparse_adj[0, 0], blocks, preferred_element_type=jnp.float32)
    partial_value = summed.astype(jnp.bfloat16).astype(jnp.float32)
    aggregated = lax.psum_scatter(
        partial_value.astype(jnp.bfloat16), "rep", scatter_dimension=0, tiled=True
    )
    pre_act = jnp.dot(aggregated, weight, preferred_element_type=jnp.float32) + bias
    sigmoid_part = jax.nn.sigmoid(pre_act)
    activated = (pre_act * sigmoid_part).astype(jnp.bfloat16)
    slope = sigmoid_part * (1.0 + pre_act * (1.0 - sigmoid_part))
    grad_pre = (cotangent.astype(jnp.float32) * slope).astype(jnp.bfloat16)
    local_weight = lax.dot_general(
        aggregated, grad_pre, (((0,), (0,)), ((), ())), preferred_element_type=jnp.float32
    )
    local_bias = jnp.sum(grad_pre.astype(jnp.float32), axis=0)
    weight_grad, bias_grad = lax.psum((local_weight, local_bias), ("row", "rep"))
    return (activated, weight_grad, bias_grad)


def solution(mesh):
    in_specs = (
        P(("row", "rep"), None),
        P(),
        P(),
        P("row", "rep", None, None, None),
        P("row", "rep", None, None, None),
        P("row", "rep", None, None),
        P("row", "rep", None),
        P("row", "rep"),
        P(("row", "rep"), None),
    )
    out_specs = (P(("row", "rep"), None), P(), P())
    return jax.shard_map(
        on_device, mesh=mesh, in_specs=in_specs, out_specs=out_specs, check_vma=False
    )
```

profile of v0, /device:TPU:1, one launch (start us, length us, event | category | flops | bytes accessed | tf_op | source)
XLA Modules:
  0.0 603.6 jit_solution(16229733063903806572)
XLA Ops:
  7.2 0.0 copy-start
  7.2 0.0 reduce-scatter.2.cloned.1.call-start
  7.2 5.0 collective-permute-start
  12.2 23.3 %collective-permute-start.2 = (bf16[128,256]{1,0:T(8,128)(2,1)}, bf16[128,256]{1,0:T(8,128)(2,1)}, u32[]{:S(2)}, u32[]{:S(2)}) collective-permute-start(bf16[128,256]{1,0:T(8,128)(2,1)} %param.9), channel_id=1, source_target_pairs={{0,1016},{8,0},{16,8},{24,16},{32,24},{40,32},{48,40},{56,48},{64,... | collective-permute-start | bytes 196616 | tf_op jit(solution)/shard_map/ppermute | solution.py:12
  35.5 16.0 %all_gather.3 = bf16[1024,256]{1,0:T(8,128)(2,1)S(1)} all-gather(bf16[128,256]{1,0:T(8,128)(2,1)} %param.9), channel_id=1, replica_groups=mesh['row'=128,'rep'=8] {'rep'}, dimensions={0}, use_global_device_ids=true | all-gather | bytes 589824 | tf_op jit(solution)/shard_map/all_gather | solution.py:41
  51.5 0.7 fusion.8
  52.2 1.5 broadcast_select_fusion
  53.7 0.0 copy-start.6
  53.7 0.8 fusion.10
  55.2 0.6 gather_fusion
  55.8 0.1 broadcast_select_fusion.1
  55.9 0.0 copy-start.2
  55.9 0.6 fusion.2
  56.5 0.2 copy-done.2
  56.8 0.3 fusion.12
  57.1 0.0 collective-permute-done
  57.1 1.9 collective-permute-start.1
  59.0 1.1 fusion.11
  60.1 11.5 %collective-permute-start.3 = (bf16[128,256]{1,0:T(8,128)(2,1)}, bf16[128,256]{1,0:T(8,128)(2,1)S(1)}, u32[]{:S(2)}, u32[]{:S(2)}) collective-permute-start(bf16[128,256]{1,0:T(8,128)(2,1)} %collective-permute-done.2), channel_id=1, source_target_pairs={{0,1016},{8,0},{16,8},{24,16},{32,24},{40,32},{48,40},{56,48},{64,... | collective-permute-start | bytes 196616 | tf_op jit(solution)/shard_map/ppermute | solution.py:12
  71.6 0.3 fusion.6
  71.9 1.1 convolution_add_fusion.1
  73.1 0.2 collective-permute-done.3
  73.3 1.1 fusion.7
  74.3 0.0 reduce-scatter.2.cloned.1.call-update
  74.4 0.0 all-reduce.2.cloned.1.call-start
  74.4 37.1 %reduce-scatter.2.cloned.1.call-done = bf16[128,256]{1,0:T(8,128)(2,1)} async-done(((bf16[1024,256]{1,0:T(8,128)(2,1)}), bf16[128,256]{1,0:T(8,128)(2,1)}) %reduce-scatter.2.cloned.1.call-update) | async-done | bytes 65552 | tf_op jit(solution)/shard_map/reduce_scatter | solution.py:48
  111.5 1.7 convert_reduce_fusion
  113.2 1.8 fusion.13
  115.0 0.0 all-reduce.2.cloned.1.call-update
  115.0 127.6 %psum.15 = f32[256]{0:T(256)} all-reduce(f32[256]{0:T(256)S(1)} %get-tuple-element.3), channel_id=1, replica_groups=mesh['row'=128,'rep'=8] {'row','rep'}, use_global_device_ids=true, to_apply=%region_3.4 | all-reduce | flops 256 | bytes 2048 | tf_op jit(solution)/shard_map/psum | solution.py:60
  242.6 352.4 %all-reduce.2.cloned.1.call-done = f32[256,256]{1,0:T(8,128)} async-done(((f32[256,256]{1,0:T(8,128)}), f32[256,256]{1,0:T(8,128)}) %all-reduce.2.cloned.1.call-update) | async-done | bytes 262160 | tf_op jit(solution)/shard_map/psum | solution.py:60
  595.1 1.7 copy.20
  (15 shorter events, 0.0 us)
Async XLA Ops:
  7.2 48.8 %copy-start = (bf16[1,1,1024,768]{3,2,1,0:T(8,128)(2,1)S(1)}, bf16[1,1,1024,768]{3,2,1,0:T(8,128)(2,1)}, u32[]{:S(2)}) copy-start(bf16[1,1,1024,768]{3,2,1,0:T(8,128)(2,1)} %param.14) | copy-start | bytes 4718596
  7.2 104.3 %reduce-scatter.2.cloned.1.call-start = ((), (), s32[]{:S(2)}) async-start(), calls=%async_computation.1 | async-start | bytes 589824 | tf_op jit(solution)/shard_map/reduce_scatter | solution.py:48
  7.2 49.8 %collective-permute-start = (bf16[128,256]{1,0:T(8,128)(2,1)}, bf16[128,256]{1,0:T(8,128)(2,1)}, u32[]{:S(2)}, u32[]{:S(2)}) collective-permute-start(bf16[128,256]{1,0:T(8,128)(2,1)} %param.9), channel_id=1, source_target_pairs={{0,8},{8,16},{16,24},{24,32},{32,40},{40,48},{48,56},{56,64},{64,7... | collective-permute-start | bytes 196616 | tf_op jit(solution)/shard_map/ppermute | solution.py:12
  12.2 47.9 %collective-permute-start.2 = (bf16[128,256]{1,0:T(8,128)(2,1)}, bf16[128,256]{1,0:T(8,128)(2,1)}, u32[]{:S(2)}, u32[]{:S(2)}) collective-permute-start(bf16[128,256]{1,0:T(8,128)(2,1)} %param.9), channel_id=1, source_target_pairs={{0,1016},{8,0},{16,8},{24,16},{32,24},{40,32},{48,40},{56,48},{64,... | collective-permute-start | bytes 196616 | tf_op jit(solution)/shard_map/ppermute | solution.py:12
  53.7 0.9 copy-start.6
  55.9 0.8 copy-start.2
  56.8 14.9 %copy-start.1 = (bf16[1,8,128,1,128]{4,2,1,0,3:T(8,128)(2,1)S(1)}, bf16[1,8,128,1,128]{4,2,1,0,3:T(8,128)(2,1)}, u32[]{:S(2)}) copy-start(bf16[1,8,128,1,128]{4,2,1,0,3:T(8,128)(2,1)} %get-tuple-element.9) | copy-start | bytes 786436
  57.1 14.6 %collective-permute-start.1 = (bf16[128,256]{1,0:T(8,128)(2,1)}, bf16[128,256]{1,0:T(8,128)(2,1)S(1)}, u32[]{:S(2)}, u32[]{:S(2)}) collective-permute-start(bf16[128,256]{1,0:T(8,128)(2,1)} %collective-permute-done), channel_id=1, source_target_pairs={{0,8},{8,16},{16,24},{24,32},{32,40},{40,48},{48,56},{56,64},{64,7... | collective-permute-start | bytes 196616 | tf_op jit(solution)/shard_map/ppermute | solution.py:12
  60.1 13.1 %collective-permute-start.3 = (bf16[128,256]{1,0:T(8,128)(2,1)}, bf16[128,256]{1,0:T(8,128)(2,1)S(1)}, u32[]{:S(2)}, u32[]{:S(2)}) collective-permute-start(bf16[128,256]{1,0:T(8,128)(2,1)} %collective-permute-done.2), channel_id=1, source_target_pairs={{0,1016},{8,0},{16,8},{24,16},{32,24},{40,32},{48,40},{56,48},{64,... | collective-permute-start | bytes 196616 | tf_op jit(solution)/shard_map/ppermute | solution.py:12
  73.3 38.2 %copy-start.3 = (bf16[256,256]{1,0:T(8,128)(2,1)S(1)}, bf16[256,256]{1,0:T(8,128)(2,1)}, u32[]{:S(2)}) copy-start(bf16[256,256]{1,0:T(8,128)(2,1)} %param.10) | copy-start | bytes 393220
  73.3 38.2 %copy-start.4 = (bf16[128,256]{1,0:T(8,128)(2,1)S(1)}, bf16[128,256]{1,0:T(8,128)(2,1)}, u32[]{:S(2)}) copy-start(bf16[128,256]{1,0:T(8,128)(2,1)} %param.17) | copy-start | bytes 196612
  73.3 38.2 %copy-start.5 = (f32[256]{0:T(256)S(1)}, f32[256]{0:T(256)}, u32[]{:S(2)}) copy-start(f32[256]{0:T(256)} %param.11) | copy-start | bytes 3076
  74.4 520.7 %all-reduce.2.cloned.1.call-start = ((), (), s32[]{:S(2)}) async-start(), calls=%async_computation.2 | async-start | bytes 524288 | tf_op jit(solution)/shard_map/psum | solution.py:60
Sparse Core Ops, SparseCore 0:
  74.5 36.9 reduce-scatter.1
  118.4 476.5 all-reduce.1
where the time goes:
time: 605 us; the launch traced here: 604 us
  waiting for transfers between devices  390 us (64%)
  blocking collectives  144 us (24%)
  starting transfers between devices  41.8 us (7%)
  between operations  14.8 us (2%)
  matrix products  7.9 us (1%)
    psum x1, waiting for transfers between devices, on_device(): lax.psum((local_weight, local_bias), ('row', 'rep'))  352 us
    psum x1, blocking collectives, on_device(): lax.psum((local_weight, local_bias), ('row', 'rep'))  128 us
    ppermute x4, starting transfers between devices, shifted(): return lax.ppermute(value, axis, pairs)  41.7 us
    reduce_scatter x1, waiting for transfers between devices, on_device(): lax.psum_scatter(partial_value.astype(jnp.bfloat16), 'rep', scatter_dimen...  37.1 us
    all_gather x1, blocking collectives, on_device(): whole_panel = lax.all_gather(features, 'rep', axis=0, tiled=True)  16 us
  transfers between devices with their start and end apart: 6, of which 3 were waited for; matrix products, arithmetic and copies ran while one was open for 1% of the time, Pallas kernels for 0%

commit v1 on v0

v1 whole, which is shorter than its diff:
```python
import jax
import jax.numpy as jnp
from jax import lax
from jax.experimental import pallas as pl
from jax.experimental.pallas import tpu as pltpu
from jax.sharding import Mesh, PartitionSpec as P

BLK = 128
ROW_STEP = 256
AXES = ("yh", "x", "z", "yl", "core")
SIZES = (2, 4, 16, 4, 2)
ROW = ("yh", "x", "z")
REP = ("yl", "core")
PLANE = ("yh", "x", "yl", "core")
DEPTH = "z"


def fetched_from(value, distance):
    count = lax.axis_size(ROW)
    return lax.ppermute(value, ROW, [(i, (i - distance) % count) for i in range(count)])


def partial_kernel(
    mask_ref, cols_ref, count_ref, f0, f1, f2, f3, f4, panel_ref, dense_ref, sparse_ref, out_ref, rhs
):
    step = pl.program_id(0)
    band = dense_ref.shape[0]
    slots = cols_ref.shape[0]

    @pl.when(step == 0)
    def _():
        for offset, ref in enumerate((f0, f1, f2, f3, f4)):
            rhs[offset * BLK : (offset + 1) * BLK, :] = ref[...]
        for slot in range(slots):
            at = (band + slot) * BLK
            block = panel_ref[cols_ref[slot]]
            rhs[at : at + BLK, :] = jnp.where(slot < count_ref[0], block, jnp.zeros_like(block))

    tiles = ROW_STEP // BLK
    lhs = []
    for offset in range(band):
        kept = []
        for tile in range(tiles):
            block = dense_ref[offset, tile * BLK : (tile + 1) * BLK, :]
            keep = mask_ref[offset, step * tiles + tile] > 0
            kept.append(jnp.where(keep, block, jnp.zeros_like(block)))
        lhs.append(jnp.concatenate(kept, axis=0))
    lhs.append(sparse_ref[...])
    out_ref[...] = jnp.dot(
        jnp.concatenate(lhs, axis=1), rhs[...], preferred_element_type=jnp.float32
    ).astype(out_ref.dtype)


def partial_sums(mask, cols, count, pieces, panel, dense, sparse):
    band, rows, width = dense.shape
    features = panel.shape[-1]
    whole = lambda shape: pl.BlockSpec(shape, lambda i: (0,) * len(shape))
    smem = pl.BlockSpec(memory_space=pltpu.SMEM)
    depth = band * width + sparse.shape[1]
    return pl.pallas_call(
        partial_kernel,
        grid=(rows // ROW_STEP,),
        out_shape=jax.ShapeDtypeStruct((rows, features), jnp.bfloat16),
        in_specs=[smem, smem, smem]
        + [whole(piece.shape) for piece in pieces]
        + [
            whole(panel.shape),
            pl.BlockSpec((band, ROW_STEP, width), lambda i: (0, i, 0)),
            pl.BlockSpec((ROW_STEP, sparse.shape[1]), lambda i: (i, 0)),
        ],
        out_specs=pl.BlockSpec((ROW_STEP, features), lambda i: (i, 0)),
        scratch_shapes=[pltpu.VMEM((depth, features), jnp.bfloat16)],
        compiler_params=pltpu.CompilerParams(vmem_limit_bytes=24 * 2**20),
        cost_estimate=pl.CostEstimate(
            flops=2 * rows * depth * features, bytes_accessed=2 * rows * depth, transcendentals=0
        ),
    )(mask, cols, count, *pieces, panel, dense, sparse)


def layer_kernel(parts_ref, weight_ref, bias_ref, cotangent_ref, out_ref, grad_ref):
    total = parts_ref[0].astype(jnp.float32)
    for share in range(1, parts_ref.shape[0]):
        total = total + parts_ref[share].astype(jnp.float32)
    aggregated = total.astype(jnp.bfloat16)
    pre_act = jnp.dot(aggregated, weight_ref[...], preferred_element_type=jnp.float32) + bias_ref[...]
    sigmoid_part = jax.nn.sigmoid(pre_act)
    out_ref[...] = (pre_act * sigmoid_part).astype(jnp.bfloat16)
    slope = sigmoid_part * (1.0 + pre_act * (1.0 - sigmoid_part))
    grad_pre = (cotangent_ref[...].astype(jnp.float32) * slope).astype(jnp.bfloat16)
    weight_grad = lax.dot_general(
        aggregated, grad_pre, (((0,), (0,)), ((), ())), preferred_element_type=jnp.float32
    )
    bias_grad = jnp.sum(grad_pre.astype(jnp.float32), axis=0, keepdims=True)
    halves, blocks = grad_ref.shape[0], grad_ref.shape[1]
    for half in range(halves):
        at = slice(half * BLK, (half + 1) * BLK)
        tile = weight_grad[:, at].reshape(blocks, 8, BLK)
        extra = jnp.broadcast_to(bias_grad[None, :, at], (blocks, 8, BLK))
        grad_ref[half] = jnp.concatenate([tile, extra], axis=1).astype(grad_ref.dtype)


def layer(parts, weight, bias, cotangent):
    rows, features = cotangent.shape
    return pl.pallas_call(
        layer_kernel,
        out_shape=(
            jax.ShapeDtypeStruct((rows, features), jnp.bfloat16),
            jax.ShapeDtypeStruct((features // BLK, features // 8, 16, BLK), jnp.bfloat16),
        ),
        compiler_params=pltpu.CompilerParams(vmem_limit_bytes=24 * 2**20),
    )(parts, weight, bias.reshape(1, features), cotangent)


def exchanged(pieces, axes):
    return lax.all_to_all(pieces, axes, 0, 0, tiled=False)


def spread(piece, axes):
    return exchanged(jnp.broadcast_to(piece[None], (lax.axis_size(axes),) + piece.shape), axes)


def summed(pieces):
    return jnp.sum(pieces.astype(jnp.float32), axis=0).astype(jnp.bfloat16)


def on_device(
    features, weight, bias, dense_adj, dense_mask, sparse_adj, sparse_cols, sparse_count, cotangent
):
    band, rows = dense_adj.shape[2], dense_adj.shape[3]
    reach = (band - 1) // 2
    width = features.shape[1]
    pieces = [
        features if offset == reach else fetched_from(features, offset - reach)
        for offset in range(band)
    ]
    panel = lax.all_gather(features, REP, axis=0, tiled=False)
    partial = partial_sums(
        dense_mask.reshape(band, rows // BLK),
        sparse_cols.reshape(-1),
        sparse_count.reshape(-1),
        pieces,
        panel,
        dense_adj[0, 0],
        sparse_adj[0, 0],
    )
    shares = lax.axis_size(REP)
    parts = exchanged(partial.reshape(shares, rows // shares, width), REP)
    activated, grads = layer(parts, weight, bias, cotangent)
    halves, blocks = grads.shape[:2]
    mine = summed(exchanged(grads.reshape((halves * blocks,) + grads.shape[2:]), PLANE))
    mine = summed(spread(mine, DEPTH))
    grads = spread(mine, PLANE).reshape(grads.shape).astype(jnp.float32)
    weight_grad = grads[:, :, :8].transpose(1, 2, 0, 3).reshape(width, width)
    bias_grad = grads[:, 0, 8].reshape(width)
    return activated, weight_grad, bias_grad


def solution(mesh):
    fine = Mesh(mesh.devices.reshape(SIZES), AXES)
    nodes = P(AXES, None)
    in_specs = (
        nodes,
        P(),
        P(),
        P(ROW, REP, None, None, None),
        P(ROW, REP, None, None, None),
        P(ROW, REP, None, None),
        P(ROW, REP, None),
        P(ROW, REP),
        nodes,
    )
    return jax.shard_map(
        on_device, mesh=fine, in_specs=in_specs, out_specs=(nodes, P(), P()), check_vma=False
    )
```

time: 605 us -> 138 us (0.23)
  waiting for transfers between devices: 390 us -> 0.01 us
  blocking collectives: 144 us -> 92.1 us
  between operations: 14.8 us -> 1.38 us
  matrix products: 7.9 us -> 0 us
  starting transfers between devices: 41.8 us -> 34.3 us
    psum x1 -> x0, waiting for transfers between devices: 352 us -> none  [on_device(): lax.psum((local_weight, local_bias), ('row', 'rep'))]
    psum x1 -> x0, blocking collectives: 128 us -> none  [on_device(): lax.psum((local_weight, local_bias), ('row', 'rep'))]
    all_to_all x0 -> x4, blocking collectives: none -> 75.7 us  [exchanged(): return lax.all_to_all(pieces, axes, 0, 0, tiled=False)]
    reduce_scatter x1 -> x0, waiting for transfers between devices: 37.1 us -> none  [on_device(): lax.psum_scatter(partial_value.astype(jnp.bfloat16), 'rep', scatter_dimen...]
    dot_general x8 -> x0, matrix products: 7.9 us -> none  [the longest x5 3.87 us: on_device(): jnp.dot(masked[offset], fetched[offset - reach], preferred_element_type=j...]
    ppermute x4, starting transfers between devices: 41.7 us -> 34.3 us  [fetched_from(): lax.ppermute(value, ROW, [(i, (i - distance) % count) for i in range(coun...]
  transfers between devices with their start and end apart: 6 -> 4, of which waited for: 3 -> 0; matrix products, arithmetic and copies ran while one was open for 1% -> 0% of each run, Pallas kernels for 0% -> 0%
where the time goes in v1:
time: 138 us; the launch traced here: 137 us
  blocking collectives  92.1 us (67%)
  starting transfers between devices  34.3 us (25%)
  local copies, waits for them, and re-layouts  6.24 us (5%)
  Pallas kernels  3.2 us (2%)
    all_to_all x4, blocking collectives, exchanged(): return lax.all_to_all(pieces, axes, 0, 0, tiled=False)  75.7 us
    ppermute x4, starting transfers between devices, fetched_from(): lax.ppermute(value, ROW, [(i, (i - distance) % count) for i in range(coun...  34.3 us
    all_gather x1, blocking collectives, on_device(): panel = lax.all_gather(features, REP, axis=0, tiled=False)  16.4 us
    unnamed x15, local copies, waits for them, and re-layouts  4.91 us
  transfers between devices with their start and end apart: 4, of which 0 were waited for; matrix products, arithmetic and copies ran while one was open for 0% of the time, Pallas kernels for 0%

profile of v1, /device:TPU:1, one launch (start us, length us, event | category | flops | bytes accessed | tf_op | source)
XLA Modules:
  0.0 137.4 jit_solution(2496408721053764570)
XLA Ops:
  0.6 26.2 %collective-permute-start.3 = (bf16[128,256]{1,0:T(8,128)(2,1)}, bf16[128,256]{1,0:T(8,128)(2,1)S(1)}, u32[]{:S(2)}, u32[]{:S(2)}) collective-permute-start(bf16[128,256]{1,0:T(8,128)(2,1)} %f2.1), channel_id=1, source_target_pairs={{0,1008},{8,1016},{16,0},{24,8},{32,16},{40,24},{48,32},{56,40},{6... | collective-permute-start | bytes 196616 | tf_op jit(solution)/shard_map/ppermute | solution.py:20
  26.9 2.2 %collective-permute-start.2 = (bf16[128,256]{1,0:T(8,128)(2,1)}, bf16[128,256]{1,0:T(8,128)(2,1)S(1)}, u32[]{:S(2)}, u32[]{:S(2)}) collective-permute-start(bf16[128,256]{1,0:T(8,128)(2,1)} %f2.1), channel_id=1, source_target_pairs={{0,1016},{8,0},{16,8},{24,16},{32,24},{40,32},{48,40},{56,48},{64,... | collective-permute-start | bytes 196616 | tf_op jit(solution)/shard_map/ppermute | solution.py:20
  29.0 3.1 %collective-permute-start.1 = (bf16[128,256]{1,0:T(8,128)(2,1)}, bf16[128,256]{1,0:T(8,128)(2,1)S(1)}, u32[]{:S(2)}, u32[]{:S(2)}) collective-permute-start(bf16[128,256]{1,0:T(8,128)(2,1)} %f2.1), channel_id=1, source_target_pairs={{0,8},{8,16},{16,24},{24,32},{32,40},{40,48},{48,56},{56,64},{64,7... | collective-permute-start | bytes 196616 | tf_op jit(solution)/shard_map/ppermute | solution.py:20
  32.2 2.8 %collective-permute-start = (bf16[128,256]{1,0:T(8,128)(2,1)}, bf16[128,256]{1,0:T(8,128)(2,1)S(1)}, u32[]{:S(2)}, u32[]{:S(2)}) collective-permute-start(bf16[128,256]{1,0:T(8,128)(2,1)} %f2.1), channel_id=1, source_target_pairs={{0,16},{8,24},{16,32},{24,40},{32,48},{40,56},{48,64},{56,72},{64,... | collective-permute-start | bytes 196616 | tf_op jit(solution)/shard_map/ppermute | solution.py:20
  35.0 16.4 %all-gather = bf16[1024,256]{1,0:T(8,128)(2,1)S(1)} all-gather(bf16[128,256]{1,0:T(8,128)(2,1)} %f2.1), channel_id=2, replica_groups=mesh['yh'=2,'x'=4,'z'=16,'yl'=4,'core'=2] {'yl','core'}, dimensions={0}, use_global_device_ids=true | all-gather | bytes 589824 | tf_op jit(solution)/shard_map/all_gather | solution.py:136
  52.1 0.7 copy.17
  52.7 0.0 collective-permute-done.3.f4
  52.7 0.0 collective-permute-done.2.f3
  52.8 0.0 collective-permute-done.1.f1
  52.8 0.0 collective-permute-done.f0
  52.8 0.0 copy-start
  52.8 1.4 %copy-done = bf16[1,1,1024,768]{3,2,1,0:T(8,128)(2,1)S(1)} copy-done((bf16[1,1,1024,768]{3,2,1,0:T(8,128)(2,1)S(1)}, bf16[1,1,1024,768]{3,2,1,0:T(8,128)(2,1)}, u32[]{:S(2)}) %copy-start) | copy-done | bytes 1572888
  54.2 0.0 copy-start.1
  54.2 1.3 copy-done.1
  55.5 0.0 copy-start.2
  55.5 0.8 copy-done.2
  56.3 0.0 copy-start.6
  56.3 0.7 copy-done.6
  57.0 0.0 copy-start.3
  57.0 0.0 copy-start.4
  57.0 2.4 %shard_map.112 = bf16[1024,256]{1,0:T(8,128)(2,1)S(1)} custom-call(s32[5,8]{1,0:T(8,128)S(1)} %bitcast.25, s32[6]{0:T(128)S(1)} %bitcast.27, s32[1]{0:T(128)} %bitcast.19.count_ref, bf16[128,256]{1,0:T(8,128)(2,1)S(1)} %collective-permute-done.f0, bf16[128,256]{1,0:T(8,128)(2,1)S(1)} %collective-permute-done.1.f1, bf16[128,256]{1,0:T(8,128)(2,1)S(1)} %copy-done.2, ...), custom_call_target="tpu_custom_call" | custom-call | flops 738197504 | bytes 2883584 | tf_op jit(solution)/shard_map/pallas_call | solution.py:60
  59.4 16.9 %all_to_all.20.parts_ref = bf16[8,128,256]{2,1,0:T(8,128)(2,1)S(1)} all-to-all(bf16[8,128,256]{2,1,0:T(8,128)(2,1)S(1)} %bitcast.21), channel_id=1, replica_groups=mesh['yh'=2,'x'=4,'z'=16,'yl'=4,'core'=2] {'yl','core'}, dimensions={0} | all-to-all | bytes 1048576 | tf_op jit(solution)/shard_map/all_to_all | solution.py:115
  76.3 0.0 copy-done.3
  76.3 0.0 copy-done.4
  76.3 0.0 copy-done.5
  76.3 0.8 shard_map.113
  77.1 21.7 %all_to_all.21 = bf16[64,16,128]{2,1,0:T(8,128)(2,1)S(1)} all-to-all(bf16[64,16,128]{2,1,0:T(8,128)(2,1)S(1)} %bitcast.24), channel_id=1, replica_groups=mesh['yh'=2,'x'=4,'z'=16,'yl'=4,'core'=2] {'yh','x','yl','core'}, dimensions={0} | all-to-all | bytes 524288 | tf_op jit(solution)/shard_map/all_to_all | solution.py:115
  98.9 0.1 reduce_sum.24
  98.9 17.9 %all_to_all.22 = bf16[16,16,128]{2,1,0:T(8,128)(2,1)S(1)} all-to-all(bf16[16,16,128]{2,1,0:T(8,128)(2,1)S(1)} %broadcast_in_dim.4), channel_id=1, replica_groups=mesh['yh'=2,'x'=4,'z'=16,'yl'=4,'core'=2] {'z'}, dimensions={0} | all-to-all | bytes 131072 | tf_op jit(solution)/shard_map/all_to_all | solution.py:115
  116.9 19.2 %all_to_all.23 = bf16[64,16,128]{2,1,0:T(8,128)(2,1)S(1)} all-to-all(bf16[64,16,128]{2,1,0:T(8,128)(2,1)S(1)} %broadcast_in_dim.5), channel_id=1, replica_groups=mesh['yh'=2,'x'=4,'z'=16,'yl'=4,'core'=2] {'yh','x','yl','core'}, dimensions={0} | all-to-all | bytes 524288 | tf_op jit(solution)/shard_map/all_to_all | solution.py:115
  136.1 0.6 slice.9
  136.7 0.7 copy_bitcast_fusion
  (5 shorter events, 0.1 us)
Async XLA Ops:
  0.6 52.1 %collective-permute-start.3 = (bf16[128,256]{1,0:T(8,128)(2,1)}, bf16[128,256]{1,0:T(8,128)(2,1)S(1)}, u32[]{:S(2)}, u32[]{:S(2)}) collective-permute-start(bf16[128,256]{1,0:T(8,128)(2,1)} %f2.1), channel_id=1, source_target_pairs={{0,1008},{8,1016},{16,0},{24,8},{32,16},{40,24},{48,32},{56,40},{6... | collective-permute-start | bytes 196616 | tf_op jit(solution)/shard_map/ppermute | solution.py:20
  26.9 25.9 %collective-permute-start.2 = (bf16[128,256]{1,0:T(8,128)(2,1)}, bf16[128,256]{1,0:T(8,128)(2,1)S(1)}, u32[]{:S(2)}, u32[]{:S(2)}) collective-permute-start(bf16[128,256]{1,0:T(8,128)(2,1)} %f2.1), channel_id=1, source_target_pairs={{0,1016},{8,0},{16,8},{24,16},{32,24},{40,32},{48,40},{56,48},{64,... | collective-permute-start | bytes 196616 | tf_op jit(solution)/shard_map/ppermute | solution.py:20
  29.0 23.7 %collective-permute-start.1 = (bf16[128,256]{1,0:T(8,128)(2,1)}, bf16[128,256]{1,0:T(8,128)(2,1)S(1)}, u32[]{:S(2)}, u32[]{:S(2)}) collective-permute-start(bf16[128,256]{1,0:T(8,128)(2,1)} %f2.1), channel_id=1, source_target_pairs={{0,8},{8,16},{16,24},{24,32},{32,40},{40,48},{48,56},{56,64},{64,7... | collective-permute-start | bytes 196616 | tf_op jit(solution)/shard_map/ppermute | solution.py:20
  32.2 20.6 %collective-permute-start = (bf16[128,256]{1,0:T(8,128)(2,1)}, bf16[128,256]{1,0:T(8,128)(2,1)S(1)}, u32[]{:S(2)}, u32[]{:S(2)}) collective-permute-start(bf16[128,256]{1,0:T(8,128)(2,1)} %f2.1), channel_id=1, source_target_pairs={{0,16},{8,24},{16,32},{24,40},{32,48},{40,56},{48,64},{56,72},{64,... | collective-permute-start | bytes 196616 | tf_op jit(solution)/shard_map/ppermute | solution.py:20
  52.8 1.4 %copy-start = (bf16[1,1,1024,768]{3,2,1,0:T(8,128)(2,1)S(1)}, bf16[1,1,1024,768]{3,2,1,0:T(8,128)(2,1)}, u32[]{:S(2)}) copy-start(bf16[1,1,1024,768]{3,2,1,0:T(8,128)(2,1)} %param.14) | copy-start | bytes 4718596
  54.2 1.3 copy-start.1
  55.5 0.8 copy-start.2
  56.3 0.7 copy-start.6
  57.0 19.3 %copy-start.3 = (bf16[256,256]{1,0:T(8,128)(2,1)S(1)}, bf16[256,256]{1,0:T(8,128)(2,1)}, u32[]{:S(2)}) copy-start(bf16[256,256]{1,0:T(8,128)(2,1)} %weight_ref.1) | copy-start | bytes 393220
  57.0 19.3 %copy-start.4 = (bf16[128,256]{1,0:T(8,128)(2,1)S(1)}, bf16[128,256]{1,0:T(8,128)(2,1)}, u32[]{:S(2)}) copy-start(bf16[128,256]{1,0:T(8,128)(2,1)} %cotangent_ref.1) | copy-start | bytes 196612
  57.0 19.3 %copy-start.5 = (f32[256]{0:T(256)S(1)}, f32[256]{0:T(256)}, u32[]{:S(2)}) copy-start(f32[256]{0:T(256)} %param.11) | copy-start | bytes 3076

commit v2 on v1

v2 whole, which is shorter than its diff:
```python
import jax
import jax.numpy as jnp
from jax import lax
from jax.experimental import pallas as pl
from jax.experimental.pallas import tpu as pltpu
from jax.sharding import Mesh, PartitionSpec as P

BLK = 128
ROW_STEP = 256
AXES = ("yh", "x", "z", "yl", "core")
SIZES = (2, 4, 16, 4, 2)
ROW = ("yh", "x", "z")
REP = ("yl", "core")
PLANE = ("yh", "x", "yl", "core")
DEPTH = "z"
SMALL = pltpu.CompilerParams(vmem_limit_bytes=8 * 2**20)


def fetched_from(value, distance):
    count = lax.axis_size(ROW)
    return lax.ppermute(value, ROW, [(i, (i - distance) % count) for i in range(count)])


def partial_kernel(
    mask_hbm, cols_hbm, count_hbm, f3, f1, f0, f4, panel_ref, dense_hbm, sparse_hbm, out_ref,
    mask, cols, count, dense, sparse, rhs, small_sems, dense_sems, sparse_sems,
):
    band, rows = dense.shape[:2]
    slots = cols.shape[-1]
    steps = rows // ROW_STEP
    small = [
        pltpu.make_async_copy(source, target, small_sems.at[i])
        for i, (source, target) in enumerate(
            ((cols_hbm, cols), (count_hbm, count), (mask_hbm, mask))
        )
    ]
    large = []
    for step in range(steps):
        at = pl.ds(step * ROW_STEP, ROW_STEP)
        large.append(
            (
                pltpu.make_async_copy(dense_hbm.at[:, at, :], dense.at[:, at, :], dense_sems.at[step]),
                pltpu.make_async_copy(sparse_hbm.at[at, :], sparse.at[at, :], sparse_sems.at[step]),
            )
        )
    for copy in small:
        copy.start()
    for pair in large:
        for copy in pair:
            copy.start()
    share = lax.axis_index("yl") * lax.axis_size("core") + lax.axis_index("core")
    for offset, ref in enumerate((f0, f1, panel_ref.at[share], f3, f4)):
        rhs[offset * BLK : (offset + 1) * BLK, :] = ref[...]
    for copy in small:
        copy.wait()
    for slot in range(slots):
        at = (band + slot) * BLK
        block = panel_ref[cols[0, 0, slot]]
        live = slot < count[0, 0]
        rhs[at : at + BLK, :] = jnp.where(live, block, jnp.zeros_like(block))
    tiles = ROW_STEP // BLK
    for step in range(steps):
        for copy in large[step]:
            copy.wait()
        lhs = []
        for offset in range(band):
            kept = []
            for tile in range(step * tiles, (step + 1) * tiles):
                block = dense[offset, tile * BLK : (tile + 1) * BLK, :]
                kept.append(jnp.where(mask[offset, 0, tile] > 0, block, jnp.zeros_like(block)))
            lhs.append(jnp.concatenate(kept, axis=0))
        at = slice(step * ROW_STEP, (step + 1) * ROW_STEP)
        lhs.append(sparse[at, :])
        out_ref[at, :] = jnp.dot(
            jnp.concatenate(lhs, axis=1), rhs[...], preferred_element_type=jnp.float32
        ).astype(out_ref.dtype)


def partial_sums(mask, cols, count, neighbours, panel, dense, sparse):
    band, rows, width = dense.shape
    features = panel.shape[-1]
    hbm = pl.BlockSpec(memory_space=pltpu.HBM)
    vmem = pl.BlockSpec(memory_space=pltpu.VMEM)
    depth = band * width + sparse.shape[1]
    steps = rows // ROW_STEP
    return pl.pallas_call(
        partial_kernel,
        out_shape=jax.ShapeDtypeStruct((rows, features), jnp.bfloat16),
        in_specs=[hbm] * 3 + [vmem] * 5 + [hbm] * 2,
        out_specs=vmem,
        scratch_shapes=[
            pltpu.SMEM(mask.shape, jnp.int32),
            pltpu.SMEM(cols.shape, jnp.int32),
            pltpu.SMEM(count.shape, jnp.int32),
            pltpu.VMEM(dense.shape, jnp.bfloat16),
            pltpu.VMEM(sparse.shape, jnp.bfloat16),
            pltpu.VMEM((depth, features), jnp.bfloat16),
            pltpu.SemaphoreType.DMA((3,)),
            pltpu.SemaphoreType.DMA((steps,)),
            pltpu.SemaphoreType.DMA((steps,)),
        ],
        compiler_params=pltpu.CompilerParams(vmem_limit_bytes=52 * 2**20),
        cost_estimate=pl.CostEstimate(
            flops=2 * rows * depth * features, bytes_accessed=2 * rows * depth, transcendentals=0
        ),
    )(mask, cols, count, *neighbours, panel, dense, sparse)


def layer_kernel(parts_ref, weight_ref, bias_ref, cotangent_ref, out_ref, grad_ref):
    aggregated = total_of(parts_ref).astype(jnp.bfloat16)
    pre_act = jnp.dot(aggregated, weight_ref[...], preferred_element_type=jnp.float32) + bias_ref[...]
    sigmoid_part = jax.nn.sigmoid(pre_act)
    out_ref[...] = (pre_act * sigmoid_part).astype(jnp.bfloat16)
    slope = sigmoid_part * (1.0 + pre_act * (1.0 - sigmoid_part))
    grad_pre = (cotangent_ref[...].astype(jnp.float32) * slope).astype(jnp.bfloat16)
    weight_grad = lax.dot_general(
        aggregated, grad_pre, (((0,), (0,)), ((), ())), preferred_element_type=jnp.float32
    )
    bias_grad = jnp.sum(grad_pre.astype(jnp.float32), axis=0, keepdims=True)
    halves, blocks = grad_ref.shape[0], grad_ref.shape[1]
    lines = [bias_grad[:, half * BLK : (half + 1) * BLK] for half in range(halves)]
    lines.append(jnp.zeros((8 - halves, BLK), jnp.float32))
    extra = jnp.broadcast_to(jnp.concatenate(lines, axis=0)[None], (blocks, 8, BLK))
    for half in range(halves):
        tile = weight_grad[:, half * BLK : (half + 1) * BLK].reshape(blocks, 8, BLK)
        grad_ref[half] = jnp.concatenate([tile, extra], axis=1).astype(grad_ref.dtype)


def layer(parts, weight, bias, cotangent):
    rows, features = cotangent.shape
    return pl.pallas_call(
        layer_kernel,
        out_shape=(
            jax.ShapeDtypeStruct((rows, features), jnp.bfloat16),
            jax.ShapeDtypeStruct((features // BLK, features // 8, 16, BLK), jnp.bfloat16),
        ),
        compiler_params=pltpu.CompilerParams(vmem_limit_bytes=16 * 2**20),
    )(parts, weight, bias.reshape(1, features), cotangent)


def total_of(parts_ref):
    total = parts_ref[0].astype(jnp.float32)
    for part in range(1, parts_ref.shape[0]):
        total = total + parts_ref[part].astype(jnp.float32)
    return total


def plane_kernel(parts_ref, out_ref):
    total = total_of(parts_ref).astype(out_ref.dtype)
    out_ref[...] = jnp.broadcast_to(total[None], out_ref.shape)


def depth_kernel(parts_ref, out_ref, bias_ref):
    total = total_of(parts_ref)
    halves = bias_ref.shape[1] // BLK
    bias_ref[...] = jnp.concatenate([total[8 + half : 9 + half] for half in range(halves)], axis=1)
    out_ref[...] = jnp.broadcast_to(total[:8].astype(out_ref.dtype)[None], out_ref.shape)


def unpack_kernel(pieces_ref, out_ref):
    for half in range(pieces_ref.shape[0]):
        tile = pieces_ref[half].astype(jnp.float32)
        out_ref[:, half * BLK : (half + 1) * BLK] = tile.reshape(out_ref.shape[0], BLK)


def exchanged(pieces, axes):
    return lax.all_to_all(pieces, axes, 0, 0, tiled=False)


def summed_over_devices(grads):
    halves, blocks, rows, _ = grads.shape
    features = halves * BLK
    plane, depth = lax.axis_size(PLANE), lax.axis_size(DEPTH)
    mine = pl.pallas_call(
        plane_kernel, out_shape=jax.ShapeDtypeStruct((depth, rows, BLK), jnp.bfloat16), compiler_params=SMALL
    )(exchanged(grads.reshape(plane, rows, BLK), PLANE))
    mine, bias_grad = pl.pallas_call(
        depth_kernel,
        out_shape=(
            jax.ShapeDtypeStruct((plane, 8, BLK), jnp.bfloat16),
            jax.ShapeDtypeStruct((1, features), jnp.float32),
        ),
        compiler_params=SMALL,
    )(exchanged(mine, DEPTH))
    weight_grad = pl.pallas_call(
        unpack_kernel,
        out_shape=jax.ShapeDtypeStruct((blocks * 8, features), jnp.float32),
        compiler_params=SMALL,
    )(exchanged(mine, PLANE).reshape(halves, blocks, 8, BLK))
    return weight_grad, bias_grad.reshape(features)


def on_device(
    features, weight, bias, dense_adj, dense_mask, sparse_adj, sparse_cols, sparse_count, cotangent
):
    band, rows = dense_adj.shape[2], dense_adj.shape[3]
    reach = (band - 1) // 2
    width = features.shape[1]
    neighbours = [fetched_from(features, k) for k in (1, -1, -2, 2)]
    panel = lax.all_gather(features, REP, axis=0, tiled=False)
    partial = partial_sums(
        dense_mask.reshape(band, 1, rows // BLK),
        sparse_cols,
        sparse_count,
        neighbours,
        panel,
        dense_adj[0, 0],
        sparse_adj[0, 0],
    )
    shares = lax.axis_size(REP)
    parts = exchanged(partial.reshape(shares, rows // shares, width), REP)
    activated, grads = layer(parts, weight, bias, cotangent)
    weight_grad, bias_grad = summed_over_devices(grads)
    return activated, weight_grad, bias_grad


def solution(mesh):
    fine = Mesh(mesh.devices.reshape(SIZES), AXES)
    nodes = P(AXES, None)
    in_specs = (
        nodes,
        P(),
        P(),
        P(ROW, REP, None, None, None),
        P(ROW, REP, None, None, None),
        P(ROW, REP, None, None),
        P(ROW, REP, None),
        P(ROW, REP),
        nodes,
    )
    return jax.shard_map(
        on_device, mesh=fine, in_specs=in_specs, out_specs=(nodes, P(), P()), check_vma=False
    )
```

time: 138 us -> 128 us (0.928)
  blocking collectives: 92.1 us -> 84.4 us
  local copies, waits for them, and re-layouts: 6.24 us -> 1.34 us
  Pallas kernels: 3.2 us -> 5.68 us
    all_to_all x4, blocking collectives: 75.7 us -> 67.9 us  [exchanged(): return lax.all_to_all(pieces, axes, 0, 0, tiled=False)]
    unnamed x15 -> x10, local copies, waits for them, and re-layouts: 4.91 us -> 1.34 us
    pallas_call x1 -> x4, Pallas kernels: 2.35 us -> 4.83 us  [the longest x1 3.45 us: partial_sums(): pl.pallas_call(partial_kernel, out_shape=jax.ShapeDtypeStruct((rows, feat...]
where the time goes in v2:
time: 128 us; the launch traced here: 127 us
  blocking collectives  84.4 us (66%)
  starting transfers between devices  34.3 us (27%)
  Pallas kernels  5.68 us (4%)
  between operations  1.37 us (1%)
  local copies, waits for them, and re-layouts  1.34 us (1%)
    all_to_all x4, blocking collectives, exchanged(): return lax.all_to_all(pieces, axes, 0, 0, tiled=False)  67.9 us
    ppermute x4, starting transfers between devices, fetched_from(): lax.ppermute(value, ROW, [(i, (i - distance) % count) for i in range(coun...  34.3 us
    all_gather x1, blocking collectives, on_device(): panel = lax.all_gather(features, REP, axis=0, tiled=False)  16.6 us
    pallas_call x1, Pallas kernels, partial_sums(): pl.pallas_call(partial_kernel, out_shape=jax.ShapeDtypeStruct((rows, feat...  3.45 us
  transfers between devices with their start and end apart: 4, of which 0 were waited for; matrix products, arithmetic and copies ran while one was open for 0% of the time, Pallas kernels for 0%

profile of v2, /device:TPU:1, one launch (start us, length us, event | category | flops | bytes accessed | tf_op | source)
XLA Modules:
  0.0 127.2 jit_solution(2125425954379676428)
XLA Ops:
  0.6 6.6 %collective-permute-start.2 = (bf16[128,256]{1,0:T(8,128)(2,1)}, bf16[128,256]{1,0:T(8,128)(2,1)S(1)}, u32[]{:S(2)}, u32[]{:S(2)}) collective-permute-start(bf16[128,256]{1,0:T(8,128)(2,1)} %param.9), channel_id=1, source_target_pairs={{0,16},{8,24},{16,32},{24,40},{32,48},{40,56},{48,64},{56,72},{64,... | collective-permute-start | bytes 196616 | tf_op jit(solution)/shard_map/ppermute | solution.py:21
  7.3 4.0 %collective-permute-start.1 = (bf16[128,256]{1,0:T(8,128)(2,1)}, bf16[128,256]{1,0:T(8,128)(2,1)S(1)}, u32[]{:S(2)}, u32[]{:S(2)}) collective-permute-start(bf16[128,256]{1,0:T(8,128)(2,1)} %param.9), channel_id=1, source_target_pairs={{0,8},{8,16},{16,24},{24,32},{32,40},{40,48},{48,56},{56,64},{64,7... | collective-permute-start | bytes 196616 | tf_op jit(solution)/shard_map/ppermute | solution.py:21
  11.3 19.4 %collective-permute-start = (bf16[128,256]{1,0:T(8,128)(2,1)}, bf16[128,256]{1,0:T(8,128)(2,1)S(1)}, u32[]{:S(2)}, u32[]{:S(2)}) collective-permute-start(bf16[128,256]{1,0:T(8,128)(2,1)} %param.9), channel_id=1, source_target_pairs={{0,1016},{8,0},{16,8},{24,16},{32,24},{40,32},{48,40},{56,48},{64,... | collective-permute-start | bytes 196616 | tf_op jit(solution)/shard_map/ppermute | solution.py:21
  30.7 4.3 %collective-permute-start.3 = (bf16[128,256]{1,0:T(8,128)(2,1)}, bf16[128,256]{1,0:T(8,128)(2,1)S(1)}, u32[]{:S(2)}, u32[]{:S(2)}) collective-permute-start(bf16[128,256]{1,0:T(8,128)(2,1)} %param.9), channel_id=1, source_target_pairs={{0,1008},{8,1016},{16,0},{24,8},{32,16},{40,24},{48,32},{56,40},{6... | collective-permute-start | bytes 196616 | tf_op jit(solution)/shard_map/ppermute | solution.py:21
  35.0 16.6 %all-gather = bf16[1024,256]{1,0:T(8,128)(2,1)S(1)} all-gather(bf16[128,256]{1,0:T(8,128)(2,1)} %param.9), channel_id=2, replica_groups=mesh['yh'=2,'x'=4,'z'=16,'yl'=4,'core'=2] {'yl','core'}, dimensions={0}, use_global_device_ids=true | all-gather | bytes 589824 | tf_op jit(solution)/shard_map/all_gather | solution.py:200
  52.2 0.0 collective-permute-done.2.f0
  52.2 0.0 collective-permute-done.1.f1
  52.2 0.0 collective-permute-done.f3
  52.2 0.0 collective-permute-done.3.f4
  52.2 0.0 copy-start.2
  52.3 0.7 copy-done.2
  52.9 0.0 copy-start.4
  52.9 0.7 copy-done.4
  53.6 0.0 copy-start
  53.6 0.0 copy-start.1
  53.6 0.0 copy-start.3
  53.6 3.5 %shard_map.112 = bf16[1024,256]{1,0:T(8,128)(2,1)S(1)} custom-call(s32[5,1,8]{2,1,0:T(1,128)S(1)} %bitcast.13, s32[1,1,6]{2,1,0:T(1,128)S(1)} %copy-done.4, s32[1,1]{1,0:T(1,128)S(6)} %copy.12.count_hbm, bf16[128,256]{1,0:T(8,128)(2,1)S(1)} %collective-permute-done.f3, bf16[128,256]{1,0:T(8,128)(2,1)S(1)} %collective-permute-done.1.f1, ...), custom_call_target="tpu_custom_call" | custom-call | flops 738197504 | bytes 2883584 | tf_op jit(solution)/shard_map/pallas_call | solution.py:86
  57.1 16.9 %all_to_all.20.parts_ref = bf16[8,128,256]{2,1,0:T(8,128)(2,1)S(1)} all-to-all(bf16[8,128,256]{2,1,0:T(8,128)(2,1)S(1)} %bitcast.10), channel_id=1, replica_groups=mesh['yh'=2,'x'=4,'z'=16,'yl'=4,'core'=2] {'yl','core'}, dimensions={0} | all-to-all | bytes 1048576 | tf_op jit(solution)/shard_map/all_to_all | solution.py:167
  73.9 0.0 copy-done
  74.0 0.0 copy-done.1
  74.0 0.0 copy-done.3
  74.0 0.8 shard_map.113
  74.8 18.7 %all_to_all.21.parts_ref = bf16[64,16,128]{2,1,0:T(8,128)(2,1)S(1)} all-to-all(bf16[64,16,128]{2,1,0:T(8,128)(2,1)S(1)} %bitcast.12), channel_id=1, replica_groups=mesh['yh'=2,'x'=4,'z'=16,'yl'=4,'core'=2] {'yh','x','yl','core'}, dimensions={0} | all-to-all | bytes 524288 | tf_op jit(solution)/shard_map/all_to_all | solution.py:167
  93.5 0.1 shard_map.114
  93.6 15.5 %all_to_all.22.parts_ref = bf16[16,16,128]{2,1,0:T(8,128)(2,1)S(1)} all-to-all(bf16[16,16,128]{2,1,0:T(8,128)(2,1)S(1)} %shard_map.114), channel_id=1, replica_groups=mesh['yh'=2,'x'=4,'z'=16,'yl'=4,'core'=2] {'z'}, dimensions={0} | all-to-all | bytes 131072 | tf_op jit(solution)/shard_map/all_to_all | solution.py:167
  109.0 0.6 shard_map.115
  109.6 16.9 %all_to_all.23 = bf16[64,8,128]{2,1,0:T(8,128)(2,1)S(1)} all-to-all(bf16[64,8,128]{2,1,0:T(8,128)(2,1)S(1)} %get-tuple-element.9), channel_id=1, replica_groups=mesh['yh'=2,'x'=4,'z'=16,'yl'=4,'core'=2] {'yh','x','yl','core'}, dimensions={0} | all-to-all | bytes 262144 | tf_op jit(solution)/shard_map/all_to_all | solution.py:167
  126.5 0.7 shard_map.116
Async XLA Ops:
  0.6 51.6 %collective-permute-start.2 = (bf16[128,256]{1,0:T(8,128)(2,1)}, bf16[128,256]{1,0:T(8,128)(2,1)S(1)}, u32[]{:S(2)}, u32[]{:S(2)}) collective-permute-start(bf16[128,256]{1,0:T(8,128)(2,1)} %param.9), channel_id=1, source_target_pairs={{0,16},{8,24},{16,32},{24,40},{32,48},{40,56},{48,64},{56,72},{64,... | collective-permute-start | bytes 196616 | tf_op jit(solution)/shard_map/ppermute | solution.py:21
  7.3 44.9 %collective-permute-start.1 = (bf16[128,256]{1,0:T(8,128)(2,1)}, bf16[128,256]{1,0:T(8,128)(2,1)S(1)}, u32[]{:S(2)}, u32[]{:S(2)}) collective-permute-start(bf16[128,256]{1,0:T(8,128)(2,1)} %param.9), channel_id=1, source_target_pairs={{0,8},{8,16},{16,24},{24,32},{32,40},{40,48},{48,56},{56,64},{64,7... | collective-permute-start | bytes 196616 | tf_op jit(solution)/shard_map/ppermute | solution.py:21
  11.3 40.9 %collective-permute-start = (bf16[128,256]{1,0:T(8,128)(2,1)}, bf16[128,256]{1,0:T(8,128)(2,1)S(1)}, u32[]{:S(2)}, u32[]{:S(2)}) collective-permute-start(bf16[128,256]{1,0:T(8,128)(2,1)} %param.9), channel_id=1, source_target_pairs={{0,1016},{8,0},{16,8},{24,16},{32,24},{40,32},{48,40},{56,48},{64,... | collective-permute-start | bytes 196616 | tf_op jit(solution)/shard_map/ppermute | solution.py:21
  30.7 21.5 %collective-permute-start.3 = (bf16[128,256]{1,0:T(8,128)(2,1)}, bf16[128,256]{1,0:T(8,128)(2,1)S(1)}, u32[]{:S(2)}, u32[]{:S(2)}) collective-permute-start(bf16[128,256]{1,0:T(8,128)(2,1)} %param.9), channel_id=1, source_target_pairs={{0,1008},{8,1016},{16,0},{24,8},{32,16},{40,24},{48,32},{56,40},{6... | collective-permute-start | bytes 196616 | tf_op jit(solution)/shard_map/ppermute | solution.py:21
  52.2 0.7 copy-start.2
  52.9 0.7 copy-start.4
  53.6 20.4 %copy-start = (bf16[256,256]{1,0:T(8,128)(2,1)S(1)}, bf16[256,256]{1,0:T(8,128)(2,1)}, u32[]{:S(2)}) copy-start(bf16[256,256]{1,0:T(8,128)(2,1)} %weight_ref.1) | copy-start | bytes 393220
  53.6 20.4 %copy-start.1 = (bf16[128,256]{1,0:T(8,128)(2,1)S(1)}, bf16[128,256]{1,0:T(8,128)(2,1)}, u32[]{:S(2)}) copy-start(bf16[128,256]{1,0:T(8,128)(2,1)} %cotangent_ref.1) | copy-start | bytes 196612
  53.6 20.4 %copy-start.3 = (f32[256]{0:T(256)S(1)}, f32[256]{0:T(256)}, u32[]{:S(2)}) copy-start(f32[256]{0:T(256)} %param.11) | copy-start | bytes 3076

commit v3 on v2

--- a/solution.py
+++ b/solution.py
@@ -117,13 +117,17 @@
         aggregated, grad_pre, (((0,), (0,)), ((), ())), preferred_element_type=jnp.float32
     )
     bias_grad = jnp.sum(grad_pre.astype(jnp.float32), axis=0, keepdims=True)
-    halves, blocks = grad_ref.shape[0], grad_ref.shape[1]
-    lines = [bias_grad[:, half * BLK : (half + 1) * BLK] for half in range(halves)]
-    lines.append(jnp.zeros((8 - halves, BLK), jnp.float32))
-    extra = jnp.broadcast_to(jnp.concatenate(lines, axis=0)[None], (blocks, 8, BLK))
+    halves = bias_grad.shape[1] // BLK
+    blocks = grad_ref.shape[0] // halves
+    extra = jnp.concatenate([bias_grad[:, h * BLK : (h + 1) * BLK] for h in range(halves)], axis=0)
+    extra = jnp.broadcast_to(extra[None], (blocks,) + extra.shape).astype(grad_ref.dtype)
     for half in range(halves):
         tile = weight_grad[:, half * BLK : (half + 1) * BLK].reshape(blocks, 8, BLK)
-        grad_ref[half] = jnp.concatenate([tile, extra], axis=1).astype(grad_ref.dtype)
+        at = slice(half * blocks, (half + 1) * blocks)
+        for pair in range(4):
+            lanes = slice(pair * BLK, (pair + 1) * BLK)
+            grad_ref[at, :, lanes] = tile[:, 2 * pair : 2 * pair + 2, :].astype(grad_ref.dtype)
+        grad_ref[at, :, 4 * BLK :] = extra
 
 
 def layer(parts, weight, bias, cotangent):
@@ -132,7 +136,7 @@
         layer_kernel,
         out_shape=(
             jax.ShapeDtypeStruct((rows, features), jnp.bfloat16),
-            jax.ShapeDtypeStruct((features // BLK, features // 8, 16, BLK), jnp.bfloat16),
+            jax.ShapeDtypeStruct((features // BLK * features // 8, 2, 5 * BLK), jnp.bfloat16),
         ),
         compiler_params=pltpu.CompilerParams(vmem_limit_bytes=16 * 2**20),
     )(parts, weight, bias.reshape(1, features), cotangent)
@@ -146,7 +150,10 @@
 
 
 def plane_kernel(parts_ref, out_ref):
-    total = total_of(parts_ref).astype(out_ref.dtype)
+    total = total_of(parts_ref)
+    lines = [total[:, at : at + BLK] for at in range(0, total.shape[1], BLK)]
+    lines.append(jnp.zeros((6, BLK), jnp.float32))
+    total = jnp.concatenate(lines, axis=0).astype(out_ref.dtype)
     out_ref[...] = jnp.broadcast_to(total[None], out_ref.shape)
 
 
@@ -168,12 +175,12 @@
 
 
 def summed_over_devices(grads):
-    halves, blocks, rows, _ = grads.shape
-    features = halves * BLK
     plane, depth = lax.axis_size(PLANE), lax.axis_size(DEPTH)
+    halves = 2
+    blocks, features = grads.shape[0] // halves, halves * BLK
     mine = pl.pallas_call(
-        plane_kernel, out_shape=jax.ShapeDtypeStruct((depth, rows, BLK), jnp.bfloat16), compiler_params=SMALL
-    )(exchanged(grads.reshape(plane, rows, BLK), PLANE))
+        plane_kernel, out_shape=jax.ShapeDtypeStruct((depth, 16, BLK), jnp.bfloat16), compiler_params=SMALL
+    )(exchanged(grads, PLANE))
     mine, bias_grad = pl.pallas_call(
         depth_kernel,
         out_shape=(

time: 128 us -> 126 us (0.984)
  blocking collectives: 84.4 us -> 82.6 us
    all_to_all x4, blocking collectives: 67.9 us -> 66.1 us  [exchanged(): return lax.all_to_all(pieces, axes, 0, 0, tiled=False)]
where the time goes in v3:
time: 126 us; the launch traced here: 125 us
  blocking collectives  82.6 us (66%)
  starting transfers between devices  34.3 us (27%)
  Pallas kernels  5.69 us (5%)
  between operations  1.37 us (1%)
  local copies, waits for them, and re-layouts  1.34 us (1%)
    all_to_all x4, blocking collectives, exchanged(): return lax.all_to_all(pieces, axes, 0, 0, tiled=False)  66.1 us
    ppermute x4, starting transfers between devices, fetched_from(): lax.ppermute(value, ROW, [(i, (i - distance) % count) for i in range(coun...  34.3 us
    all_gather x1, blocking collectives, on_device(): panel = lax.all_gather(features, REP, axis=0, tiled=False)  16.6 us
    pallas_call x1, Pallas kernels, partial_sums(): pl.pallas_call(partial_kernel, out_shape=jax.ShapeDtypeStruct((rows, feat...  3.45 us
  transfers between devices with their start and end apart: 4, of which 0 were waited for; matrix products, arithmetic and copies ran while one was open for 0% of the time, Pallas kernels for 0%

profile of v3, /device:TPU:1, one launch (start us, length us, event | category | flops | bytes accessed | tf_op | source)
XLA Modules:
  0.0 125.4 jit_solution(5190836806177015542)
XLA Ops:
  0.6 6.6 %collective-permute-start.2 = (bf16[128,256]{1,0:T(8,128)(2,1)}, bf16[128,256]{1,0:T(8,128)(2,1)S(1)}, u32[]{:S(2)}, u32[]{:S(2)}) collective-permute-start(bf16[128,256]{1,0:T(8,128)(2,1)} %param.9), channel_id=1, source_target_pairs={{0,16},{8,24},{16,32},{24,40},{32,48},{40,56},{48,64},{56,72},{64,... | collective-permute-start | bytes 196616 | tf_op jit(solution)/shard_map/ppermute | solution.py:21
  7.3 4.0 %collective-permute-start.1 = (bf16[128,256]{1,0:T(8,128)(2,1)}, bf16[128,256]{1,0:T(8,128)(2,1)S(1)}, u32[]{:S(2)}, u32[]{:S(2)}) collective-permute-start(bf16[128,256]{1,0:T(8,128)(2,1)} %param.9), channel_id=1, source_target_pairs={{0,8},{8,16},{16,24},{24,32},{32,40},{40,48},{48,56},{56,64},{64,7... | collective-permute-start | bytes 196616 | tf_op jit(solution)/shard_map/ppermute | solution.py:21
  11.3 19.4 %collective-permute-start = (bf16[128,256]{1,0:T(8,128)(2,1)}, bf16[128,256]{1,0:T(8,128)(2,1)S(1)}, u32[]{:S(2)}, u32[]{:S(2)}) collective-permute-start(bf16[128,256]{1,0:T(8,128)(2,1)} %param.9), channel_id=1, source_target_pairs={{0,1016},{8,0},{16,8},{24,16},{32,24},{40,32},{48,40},{56,48},{64,... | collective-permute-start | bytes 196616 | tf_op jit(solution)/shard_map/ppermute | solution.py:21
  30.7 4.3 %collective-permute-start.3 = (bf16[128,256]{1,0:T(8,128)(2,1)}, bf16[128,256]{1,0:T(8,128)(2,1)S(1)}, u32[]{:S(2)}, u32[]{:S(2)}) collective-permute-start(bf16[128,256]{1,0:T(8,128)(2,1)} %param.9), channel_id=1, source_target_pairs={{0,1008},{8,1016},{16,0},{24,8},{32,16},{40,24},{48,32},{56,40},{6... | collective-permute-start | bytes 196616 | tf_op jit(solution)/shard_map/ppermute | solution.py:21
  35.0 16.6 %all-gather = bf16[1024,256]{1,0:T(8,128)(2,1)S(1)} all-gather(bf16[128,256]{1,0:T(8,128)(2,1)} %param.9), channel_id=2, replica_groups=mesh['yh'=2,'x'=4,'z'=16,'yl'=4,'core'=2] {'yl','core'}, dimensions={0}, use_global_device_ids=true | all-gather | bytes 589824 | tf_op jit(solution)/shard_map/all_gather | solution.py:207
  52.2 0.0 collective-permute-done.2.f0
  52.2 0.0 collective-permute-done.1.f1
  52.2 0.0 collective-permute-done.f3
  52.2 0.0 collective-permute-done.3.f4
  52.2 0.0 copy-start.2
  52.3 0.7 copy-done.2
  52.9 0.0 copy-start.4
  52.9 0.7 copy-done.4
  53.6 0.0 copy-start
  53.6 0.0 copy-start.1
  53.6 0.0 copy-start.3
  53.6 3.5 %shard_map.112 = bf16[1024,256]{1,0:T(8,128)(2,1)S(1)} custom-call(s32[5,1,8]{2,1,0:T(1,128)S(1)} %bitcast.11, s32[1,1,6]{2,1,0:T(1,128)S(1)} %copy-done.4, s32[1,1]{1,0:T(1,128)S(6)} %copy.12.count_hbm, bf16[128,256]{1,0:T(8,128)(2,1)S(1)} %collective-permute-done.f3, bf16[128,256]{1,0:T(8,128)(2,1)S(1)} %collective-permute-done.1.f1, ...), custom_call_target="tpu_custom_call" | custom-call | flops 738197504 | bytes 2883584 | tf_op jit(solution)/shard_map/pallas_call | solution.py:86
  57.1 16.9 %all_to_all.20.parts_ref = bf16[8,128,256]{2,1,0:T(8,128)(2,1)S(1)} all-to-all(bf16[8,128,256]{2,1,0:T(8,128)(2,1)S(1)} %bitcast.9), channel_id=1, replica_groups=mesh['yh'=2,'x'=4,'z'=16,'yl'=4,'core'=2] {'yl','core'}, dimensions={0} | all-to-all | bytes 1048576 | tf_op jit(solution)/shard_map/all_to_all | solution.py:174
  73.9 0.0 copy-done
  74.0 0.0 copy-done.1
  74.0 0.0 copy-done.3
  74.0 0.8 shard_map.113
  74.8 16.9 %all_to_all.21.parts_ref = bf16[64,2,640]{2,1,0:T(2,128)(2,1)S(1)} all-to-all(bf16[64,2,640]{2,1,0:T(2,128)(2,1)S(1)} %get-tuple-element.8), channel_id=1, replica_groups=mesh['yh'=2,'x'=4,'z'=16,'yl'=4,'core'=2] {'yh','x','yl','core'}, dimensions={0} | all-to-all | bytes 327680 | tf_op jit(solution)/shard_map/all_to_all | solution.py:174
  91.7 0.1 shard_map.114
  91.7 15.5 %all_to_all.22.parts_ref = bf16[16,16,128]{2,1,0:T(8,128)(2,1)S(1)} all-to-all(bf16[16,16,128]{2,1,0:T(8,128)(2,1)S(1)} %shard_map.114), channel_id=1, replica_groups=mesh['yh'=2,'x'=4,'z'=16,'yl'=4,'core'=2] {'z'}, dimensions={0} | all-to-all | bytes 131072 | tf_op jit(solution)/shard_map/all_to_all | solution.py:174
  107.2 0.6 shard_map.115
  107.8 16.9 %all_to_all.23 = bf16[64,8,128]{2,1,0:T(8,128)(2,1)S(1)} all-to-all(bf16[64,8,128]{2,1,0:T(8,128)(2,1)S(1)} %get-tuple-element.9), channel_id=1, replica_groups=mesh['yh'=2,'x'=4,'z'=16,'yl'=4,'core'=2] {'yh','x','yl','core'}, dimensions={0} | all-to-all | bytes 262144 | tf_op jit(solution)/shard_map/all_to_all | solution.py:174
  124.7 0.7 shard_map.116
Async XLA Ops:
  0.6 51.6 %collective-permute-start.2 = (bf16[128,256]{1,0:T(8,128)(2,1)}, bf16[128,256]{1,0:T(8,128)(2,1)S(1)}, u32[]{:S(2)}, u32[]{:S(2)}) collective-permute-start(bf16[128,256]{1,0:T(8,128)(2,1)} %param.9), channel_id=1, source_target_pairs={{0,16},{8,24},{16,32},{24,40},{32,48},{40,56},{48,64},{56,72},{64,... | collective-permute-start | bytes 196616 | tf_op jit(solution)/shard_map/ppermute | solution.py:21
  7.3 44.9 %collective-permute-start.1 = (bf16[128,256]{1,0:T(8,128)(2,1)}, bf16[128,256]{1,0:T(8,128)(2,1)S(1)}, u32[]{:S(2)}, u32[]{:S(2)}) collective-permute-start(bf16[128,256]{1,0:T(8,128)(2,1)} %param.9), channel_id=1, source_target_pairs={{0,8},{8,16},{16,24},{24,32},{32,40},{40,48},{48,56},{56,64},{64,7... | collective-permute-start | bytes 196616 | tf_op jit(solution)/shard_map/ppermute | solution.py:21
  11.3 40.9 %collective-permute-start = (bf16[128,256]{1,0:T(8,128)(2,1)}, bf16[128,256]{1,0:T(8,128)(2,1)S(1)}, u32[]{:S(2)}, u32[]{:S(2)}) collective-permute-start(bf16[128,256]{1,0:T(8,128)(2,1)} %param.9), channel_id=1, source_target_pairs={{0,1016},{8,0},{16,8},{24,16},{32,24},{40,32},{48,40},{56,48},{64,... | collective-permute-start | bytes 196616 | tf_op jit(solution)/shard_map/ppermute | solution.py:21
  30.7 21.5 %collective-permute-start.3 = (bf16[128,256]{1,0:T(8,128)(2,1)}, bf16[128,256]{1,0:T(8,128)(2,1)S(1)}, u32[]{:S(2)}, u32[]{:S(2)}) collective-permute-start(bf16[128,256]{1,0:T(8,128)(2,1)} %param.9), channel_id=1, source_target_pairs={{0,1008},{8,1016},{16,0},{24,8},{32,16},{40,24},{48,32},{56,40},{6... | collective-permute-start | bytes 196616 | tf_op jit(solution)/shard_map/ppermute | solution.py:21
  52.2 0.7 copy-start.2
  52.9 0.7 copy-start.4
  53.6 20.4 %copy-start = (bf16[256,256]{1,0:T(8,128)(2,1)S(1)}, bf16[256,256]{1,0:T(8,128)(2,1)}, u32[]{:S(2)}) copy-start(bf16[256,256]{1,0:T(8,128)(2,1)} %weight_ref.1) | copy-start | bytes 393220
  53.6 20.4 %copy-start.1 = (bf16[128,256]{1,0:T(8,128)(2,1)S(1)}, bf16[128,256]{1,0:T(8,128)(2,1)}, u32[]{:S(2)}) copy-start(bf16[128,256]{1,0:T(8,128)(2,1)} %cotangent_ref.1) | copy-start | bytes 196612
  53.6 20.4 %copy-start.3 = (f32[256]{0:T(256)S(1)}, f32[256]{0:T(256)}, u32[]{:S(2)}) copy-start(f32[256]{0:T(256)} %param.11) | copy-start | bytes 3076

commit v4 on v3

--- a/solution.py
+++ b/solution.py
@@ -150,18 +150,17 @@
 
 
 def plane_kernel(parts_ref, out_ref):
-    total = total_of(parts_ref)
-    lines = [total[:, at : at + BLK] for at in range(0, total.shape[1], BLK)]
-    lines.append(jnp.zeros((6, BLK), jnp.float32))
-    total = jnp.concatenate(lines, axis=0).astype(out_ref.dtype)
+    total = total_of(parts_ref).astype(out_ref.dtype)
     out_ref[...] = jnp.broadcast_to(total[None], out_ref.shape)
 
 
 def depth_kernel(parts_ref, out_ref, bias_ref):
     total = total_of(parts_ref)
-    halves = bias_ref.shape[1] // BLK
-    bias_ref[...] = jnp.concatenate([total[8 + half : 9 + half] for half in range(halves)], axis=1)
-    out_ref[...] = jnp.broadcast_to(total[:8].astype(out_ref.dtype)[None], out_ref.shape)
+    pairs = out_ref.shape[1] // 2
+    bias = total[:, pairs * BLK :]
+    bias_ref[...] = jnp.concatenate([bias[half : half + 1] for half in range(bias.shape[0])], axis=1)
+    tile = jnp.concatenate([total[:, pair * BLK : (pair + 1) * BLK] for pair in range(pairs)], axis=0)
+    out_ref[...] = jnp.broadcast_to(tile.astype(out_ref.dtype)[None], out_ref.shape)
 
 
 def unpack_kernel(pieces_ref, out_ref):
@@ -179,7 +178,7 @@
     halves = 2
     blocks, features = grads.shape[0] // halves, halves * BLK
     mine = pl.pallas_call(
-        plane_kernel, out_shape=jax.ShapeDtypeStruct((depth, 16, BLK), jnp.bfloat16), compiler_params=SMALL
+        plane_kernel, out_shape=jax.ShapeDtypeStruct((depth,) + grads.shape[1:], jnp.bfloat16), compiler_params=SMALL
     )(exchanged(grads, PLANE))
     mine, bias_grad = pl.pallas_call(
         depth_kernel,

time: 126 us -> 125 us (level)
  no operation moved by 1% of the time
where the time goes in v4:
time: 125 us
  blocking collectives  82.2 us (66%)
  starting transfers between devices  34.3 us (27%)
  Pallas kernels  5.68 us (5%)
  between operations  1.37 us (1%)
  local copies, waits for them, and re-layouts  1.34 us (1%)
    all_to_all x4, blocking collectives, exchanged(): return lax.all_to_all(pieces, axes, 0, 0, tiled=False)  65.6 us
    ppermute x4, starting transfers between devices, fetched_from(): lax.ppermute(value, ROW, [(i, (i - distance) % count) for i in range(coun...  34.3 us
    all_gather x1, blocking collectives, on_device(): panel = lax.all_gather(features, REP, axis=0, tiled=False)  16.6 us
    pallas_call x1, Pallas kernels, partial_sums(): pl.pallas_call(partial_kernel, out_shape=jax.ShapeDtypeStruct((rows, feat...  3.45 us
  transfers between devices with their start and end apart: 4, of which 0 were waited for; matrix products, arithmetic and copies ran while one was open for 0% of the time, Pallas kernels for 0%

profile of v4, /device:TPU:1, one launch (start us, length us, event | category | flops | bytes accessed | tf_op | source)
XLA Modules:
  0.0 124.9 jit_solution(12116080680443392551)
XLA Ops:
  0.6 6.6 %collective-permute-start.2 = (bf16[128,256]{1,0:T(8,128)(2,1)}, bf16[128,256]{1,0:T(8,128)(2,1)S(1)}, u32[]{:S(2)}, u32[]{:S(2)}) collective-permute-start(bf16[128,256]{1,0:T(8,128)(2,1)} %param.9), channel_id=1, source_target_pairs={{0,16},{8,24},{16,32},{24,40},{32,48},{40,56},{48,64},{56,72},{64,... | collective-permute-start | bytes 196616 | tf_op jit(solution)/shard_map/ppermute | solution.py:21
  7.3 4.0 %collective-permute-start.1 = (bf16[128,256]{1,0:T(8,128)(2,1)}, bf16[128,256]{1,0:T(8,128)(2,1)S(1)}, u32[]{:S(2)}, u32[]{:S(2)}) collective-permute-start(bf16[128,256]{1,0:T(8,128)(2,1)} %param.9), channel_id=1, source_target_pairs={{0,8},{8,16},{16,24},{24,32},{32,40},{40,48},{48,56},{56,64},{64,7... | collective-permute-start | bytes 196616 | tf_op jit(solution)/shard_map/ppermute | solution.py:21
  11.3 19.4 %collective-permute-start = (bf16[128,256]{1,0:T(8,128)(2,1)}, bf16[128,256]{1,0:T(8,128)(2,1)S(1)}, u32[]{:S(2)}, u32[]{:S(2)}) collective-permute-start(bf16[128,256]{1,0:T(8,128)(2,1)} %param.9), channel_id=1, source_target_pairs={{0,1016},{8,0},{16,8},{24,16},{32,24},{40,32},{48,40},{56,48},{64,... | collective-permute-start | bytes 196616 | tf_op jit(solution)/shard_map/ppermute | solution.py:21
  30.7 4.3 %collective-permute-start.3 = (bf16[128,256]{1,0:T(8,128)(2,1)}, bf16[128,256]{1,0:T(8,128)(2,1)S(1)}, u32[]{:S(2)}, u32[]{:S(2)}) collective-permute-start(bf16[128,256]{1,0:T(8,128)(2,1)} %param.9), channel_id=1, source_target_pairs={{0,1008},{8,1016},{16,0},{24,8},{32,16},{40,24},{48,32},{56,40},{6... | collective-permute-start | bytes 196616 | tf_op jit(solution)/shard_map/ppermute | solution.py:21
  35.0 16.6 %all-gather = bf16[1024,256]{1,0:T(8,128)(2,1)S(1)} all-gather(bf16[128,256]{1,0:T(8,128)(2,1)} %param.9), channel_id=2, replica_groups=mesh['yh'=2,'x'=4,'z'=16,'yl'=4,'core'=2] {'yl','core'}, dimensions={0}, use_global_device_ids=true | all-gather | bytes 589824 | tf_op jit(solution)/shard_map/all_gather | solution.py:206
  52.2 0.0 collective-permute-done.2.f0
  52.2 0.0 collective-permute-done.1.f1
  52.2 0.0 collective-permute-done.f3
  52.2 0.0 collective-permute-done.3.f4
  52.2 0.0 copy-start.2
  52.3 0.7 copy-done.2
  52.9 0.0 copy-start.4
  52.9 0.7 copy-done.4
  53.6 0.0 copy-start
  53.6 0.0 copy-start.1
  53.6 0.0 copy-start.3
  53.6 3.5 %shard_map.112 = bf16[1024,256]{1,0:T(8,128)(2,1)S(1)} custom-call(s32[5,1,8]{2,1,0:T(1,128)S(1)} %bitcast.11, s32[1,1,6]{2,1,0:T(1,128)S(1)} %copy-done.4, s32[1,1]{1,0:T(1,128)S(6)} %copy.12.count_hbm, bf16[128,256]{1,0:T(8,128)(2,1)S(1)} %collective-permute-done.f3, bf16[128,256]{1,0:T(8,128)(2,1)S(1)} %collective-permute-done.1.f1, ...), custom_call_target="tpu_custom_call" | custom-call | flops 738197504 | bytes 2883584 | tf_op jit(solution)/shard_map/pallas_call | solution.py:86
  57.1 16.9 %all_to_all.20.parts_ref = bf16[8,128,256]{2,1,0:T(8,128)(2,1)S(1)} all-to-all(bf16[8,128,256]{2,1,0:T(8,128)(2,1)S(1)} %bitcast.9), channel_id=1, replica_groups=mesh['yh'=2,'x'=4,'z'=16,'yl'=4,'core'=2] {'yl','core'}, dimensions={0} | all-to-all | bytes 1048576 | tf_op jit(solution)/shard_map/all_to_all | solution.py:173
  73.9 0.0 copy-done
  74.0 0.0 copy-done.1
  74.0 0.0 copy-done.3
  74.0 0.8 shard_map.113
  74.8 16.9 %all_to_all.21.parts_ref = bf16[64,2,640]{2,1,0:T(2,128)(2,1)S(1)} all-to-all(bf16[64,2,640]{2,1,0:T(2,128)(2,1)S(1)} %get-tuple-element.8), channel_id=1, replica_groups=mesh['yh'=2,'x'=4,'z'=16,'yl'=4,'core'=2] {'yh','x','yl','core'}, dimensions={0} | all-to-all | bytes 327680 | tf_op jit(solution)/shard_map/all_to_all | solution.py:173
  91.7 0.1 shard_map.114
  91.7 15.4 %all_to_all.22.parts_ref = bf16[16,2,640]{2,1,0:T(2,128)(2,1)S(1)} all-to-all(bf16[16,2,640]{2,1,0:T(2,128)(2,1)S(1)} %shard_map.114), channel_id=1, replica_groups=mesh['yh'=2,'x'=4,'z'=16,'yl'=4,'core'=2] {'z'}, dimensions={0} | all-to-all | bytes 81920 | tf_op jit(solution)/shard_map/all_to_all | solution.py:173
  107.1 0.6 shard_map.115
  107.7 16.5 %all_to_all.23 = bf16[64,8,128]{2,1,0:T(8,128)(2,1)S(1)} all-to-all(bf16[64,8,128]{2,1,0:T(8,128)(2,1)S(1)} %get-tuple-element.9), channel_id=1, replica_groups=mesh['yh'=2,'x'=4,'z'=16,'yl'=4,'core'=2] {'yh','x','yl','core'}, dimensions={0} | all-to-all | bytes 262144 | tf_op jit(solution)/shard_map/all_to_all | solution.py:173
  124.2 0.7 shard_map.116
Async XLA Ops:
  0.6 51.6 %collective-permute-start.2 = (bf16[128,256]{1,0:T(8,128)(2,1)}, bf16[128,256]{1,0:T(8,128)(2,1)S(1)}, u32[]{:S(2)}, u32[]{:S(2)}) collective-permute-start(bf16[128,256]{1,0:T(8,128)(2,1)} %param.9), channel_id=1, source_target_pairs={{0,16},{8,24},{16,32},{24,40},{32,48},{40,56},{48,64},{56,72},{64,... | collective-permute-start | bytes 196616 | tf_op jit(solution)/shard_map/ppermute | solution.py:21
  7.3 44.9 %collective-permute-start.1 = (bf16[128,256]{1,0:T(8,128)(2,1)}, bf16[128,256]{1,0:T(8,128)(2,1)S(1)}, u32[]{:S(2)}, u32[]{:S(2)}) collective-permute-start(bf16[128,256]{1,0:T(8,128)(2,1)} %param.9), channel_id=1, source_target_pairs={{0,8},{8,16},{16,24},{24,32},{32,40},{40,48},{48,56},{56,64},{64,7... | collective-permute-start | bytes 196616 | tf_op jit(solution)/shard_map/ppermute | solution.py:21
  11.3 40.9 %collective-permute-start = (bf16[128,256]{1,0:T(8,128)(2,1)}, bf16[128,256]{1,0:T(8,128)(2,1)S(1)}, u32[]{:S(2)}, u32[]{:S(2)}) collective-permute-start(bf16[128,256]{1,0:T(8,128)(2,1)} %param.9), channel_id=1, source_target_pairs={{0,1016},{8,0},{16,8},{24,16},{32,24},{40,32},{48,40},{56,48},{64,... | collective-permute-start | bytes 196616 | tf_op jit(solution)/shard_map/ppermute | solution.py:21
  30.7 21.5 %collective-permute-start.3 = (bf16[128,256]{1,0:T(8,128)(2,1)}, bf16[128,256]{1,0:T(8,128)(2,1)S(1)}, u32[]{:S(2)}, u32[]{:S(2)}) collective-permute-start(bf16[128,256]{1,0:T(8,128)(2,1)} %param.9), channel_id=1, source_target_pairs={{0,1008},{8,1016},{16,0},{24,8},{32,16},{40,24},{48,32},{56,40},{6... | collective-permute-start | bytes 196616 | tf_op jit(solution)/shard_map/ppermute | solution.py:21
  52.2 0.7 copy-start.2
  52.9 0.7 copy-start.4
  53.6 20.4 %copy-start = (bf16[256,256]{1,0:T(8,128)(2,1)S(1)}, bf16[256,256]{1,0:T(8,128)(2,1)}, u32[]{:S(2)}) copy-start(bf16[256,256]{1,0:T(8,128)(2,1)} %weight_ref.1) | copy-start | bytes 393220
  53.6 20.4 %copy-start.1 = (bf16[128,256]{1,0:T(8,128)(2,1)S(1)}, bf16[128,256]{1,0:T(8,128)(2,1)}, u32[]{:S(2)}) copy-start(bf16[128,256]{1,0:T(8,128)(2,1)} %cotangent_ref.1) | copy-start | bytes 196612
  53.6 20.4 %copy-start.3 = (f32[256]{0:T(256)S(1)}, f32[256]{0:T(256)}, u32[]{:S(2)}) copy-start(f32[256]{0:T(256)} %param.11) | copy-start | bytes 3076

commit v5 on v4

--- a/solution.py
+++ b/solution.py
@@ -6,7 +6,7 @@
 from jax.sharding import Mesh, PartitionSpec as P
 
 BLK = 128
-ROW_STEP = 256
+ROW_STEP = 512
 AXES = ("yh", "x", "z", "yl", "core")
 SIZES = (2, 4, 16, 4, 2)
 ROW = ("yh", "x", "z")
@@ -43,9 +43,11 @@
                 pltpu.make_async_copy(sparse_hbm.at[at, :], sparse.at[at, :], sparse_sems.at[step]),
             )
         )
+    for copy in large[0]:
+        copy.start()
     for copy in small:
         copy.start()
-    for pair in large:
+    for pair in large[1:]:
         for copy in pair:
             copy.start()
     share = lax.axis_index("yl") * lax.axis_size("core") + lax.axis_index("core")

time: 125 us -> 125 us (level)
  no operation moved by 1% of the time
where the time goes in v5:
time: 125 us
  blocking collectives  82.2 us (66%)
  starting transfers between devices  34.3 us (27%)
  Pallas kernels  5.58 us (4%)
  between operations  1.37 us (1%)
  local copies, waits for them, and re-layouts  1.34 us (1%)
    all_to_all x4, blocking collectives, exchanged(): return lax.all_to_all(pieces, axes, 0, 0, tiled=False)  65.6 us
    ppermute x4, starting transfers between devices, fetched_from(): lax.ppermute(value, ROW, [(i, (i - distance) % count) for i in range(coun...  34.3 us
    all_gather x1, blocking collectives, on_device(): panel = lax.all_gather(features, REP, axis=0, tiled=False)  16.6 us
    pallas_call x1, Pallas kernels, partial_sums(): pl.pallas_call(partial_kernel, out_shape=jax.ShapeDtypeStruct((rows, feat...  3.35 us
  transfers between devices with their start and end apart: 4, of which 0 were waited for; matrix products, arithmetic and copies ran while one was open for 0% of the time, Pallas kernels for 0%

profile of v5, /device:TPU:1, one launch (start us, length us, event | category | flops | bytes accessed | tf_op | source)
XLA Modules:
  0.0 124.8 jit_solution(18056453147240391847)
XLA Ops:
  0.6 6.6 %collective-permute-start.2 = (bf16[128,256]{1,0:T(8,128)(2,1)}, bf16[128,256]{1,0:T(8,128)(2,1)S(1)}, u32[]{:S(2)}, u32[]{:S(2)}) collective-permute-start(bf16[128,256]{1,0:T(8,128)(2,1)} %param.9), channel_id=1, source_target_pairs={{0,16},{8,24},{16,32},{24,40},{32,48},{40,56},{48,64},{56,72},{64,... | collective-permute-start | bytes 196616 | tf_op jit(solution)/shard_map/ppermute | solution.py:21
  7.3 4.0 %collective-permute-start.1 = (bf16[128,256]{1,0:T(8,128)(2,1)}, bf16[128,256]{1,0:T(8,128)(2,1)S(1)}, u32[]{:S(2)}, u32[]{:S(2)}) collective-permute-start(bf16[128,256]{1,0:T(8,128)(2,1)} %param.9), channel_id=1, source_target_pairs={{0,8},{8,16},{16,24},{24,32},{32,40},{40,48},{48,56},{56,64},{64,7... | collective-permute-start | bytes 196616 | tf_op jit(solution)/shard_map/ppermute | solution.py:21
  11.3 19.4 %collective-permute-start = (bf16[128,256]{1,0:T(8,128)(2,1)}, bf16[128,256]{1,0:T(8,128)(2,1)S(1)}, u32[]{:S(2)}, u32[]{:S(2)}) collective-permute-start(bf16[128,256]{1,0:T(8,128)(2,1)} %param.9), channel_id=1, source_target_pairs={{0,1016},{8,0},{16,8},{24,16},{32,24},{40,32},{48,40},{56,48},{64,... | collective-permute-start | bytes 196616 | tf_op jit(solution)/shard_map/ppermute | solution.py:21
  30.7 4.3 %collective-permute-start.3 = (bf16[128,256]{1,0:T(8,128)(2,1)}, bf16[128,256]{1,0:T(8,128)(2,1)S(1)}, u32[]{:S(2)}, u32[]{:S(2)}) collective-permute-start(bf16[128,256]{1,0:T(8,128)(2,1)} %param.9), channel_id=1, source_target_pairs={{0,1008},{8,1016},{16,0},{24,8},{32,16},{40,24},{48,32},{56,40},{6... | collective-permute-start | bytes 196616 | tf_op jit(solution)/shard_map/ppermute | solution.py:21
  35.0 16.6 %all-gather = bf16[1024,256]{1,0:T(8,128)(2,1)S(1)} all-gather(bf16[128,256]{1,0:T(8,128)(2,1)} %param.9), channel_id=2, replica_groups=mesh['yh'=2,'x'=4,'z'=16,'yl'=4,'core'=2] {'yl','core'}, dimensions={0}, use_global_device_ids=true | all-gather | bytes 589824 | tf_op jit(solution)/shard_map/all_gather | solution.py:208
  52.2 0.0 collective-permute-done.2.f0
  52.2 0.0 collective-permute-done.1.f1
  52.2 0.0 collective-permute-done.f3
  52.2 0.0 collective-permute-done.3.f4
  52.2 0.0 copy-start.2
  52.3 0.7 copy-done.2
  52.9 0.0 copy-start.4
  52.9 0.7 copy-done.4
  53.6 0.0 copy-start
  53.6 0.0 copy-start.1
  53.6 0.0 copy-start.3
  53.6 3.4 %shard_map.112 = bf16[1024,256]{1,0:T(8,128)(2,1)S(1)} custom-call(s32[5,1,8]{2,1,0:T(1,128)S(1)} %bitcast.11, s32[1,1,6]{2,1,0:T(1,128)S(1)} %copy-done.4, s32[1,1]{1,0:T(1,128)S(6)} %copy.12.count_hbm, bf16[128,256]{1,0:T(8,128)(2,1)S(1)} %collective-permute-done.f3, bf16[128,256]{1,0:T(8,128)(2,1)S(1)} %collective-permute-done.1.f1, ...), custom_call_target="tpu_custom_call" | custom-call | flops 738197504 | bytes 2883584 | tf_op jit(solution)/shard_map/pallas_call | solution.py:88
  57.0 16.9 %all_to_all.20.parts_ref = bf16[8,128,256]{2,1,0:T(8,128)(2,1)S(1)} all-to-all(bf16[8,128,256]{2,1,0:T(8,128)(2,1)S(1)} %bitcast.9), channel_id=1, replica_groups=mesh['yh'=2,'x'=4,'z'=16,'yl'=4,'core'=2] {'yl','core'}, dimensions={0} | all-to-all | bytes 1048576 | tf_op jit(solution)/shard_map/all_to_all | solution.py:175
  73.8 0.0 copy-done
  73.9 0.0 copy-done.1
  73.9 0.0 copy-done.3
  73.9 0.8 shard_map.113
  74.7 16.9 %all_to_all.21.parts_ref = bf16[64,2,640]{2,1,0:T(2,128)(2,1)S(1)} all-to-all(bf16[64,2,640]{2,1,0:T(2,128)(2,1)S(1)} %get-tuple-element.8), channel_id=1, replica_groups=mesh['yh'=2,'x'=4,'z'=16,'yl'=4,'core'=2] {'yh','x','yl','core'}, dimensions={0} | all-to-all | bytes 327680 | tf_op jit(solution)/shard_map/all_to_all | solution.py:175
  91.6 0.1 shard_map.114
  91.6 15.4 %all_to_all.22.parts_ref = bf16[16,2,640]{2,1,0:T(2,128)(2,1)S(1)} all-to-all(bf16[16,2,640]{2,1,0:T(2,128)(2,1)S(1)} %shard_map.114), channel_id=1, replica_groups=mesh['yh'=2,'x'=4,'z'=16,'yl'=4,'core'=2] {'z'}, dimensions={0} | all-to-all | bytes 81920 | tf_op jit(solution)/shard_map/all_to_all | solution.py:175
  107.0 0.6 shard_map.115
  107.6 16.5 %all_to_all.23 = bf16[64,8,128]{2,1,0:T(8,128)(2,1)S(1)} all-to-all(bf16[64,8,128]{2,1,0:T(8,128)(2,1)S(1)} %get-tuple-element.9), channel_id=1, replica_groups=mesh['yh'=2,'x'=4,'z'=16,'yl'=4,'core'=2] {'yh','x','yl','core'}, dimensions={0} | all-to-all | bytes 262144 | tf_op jit(solution)/shard_map/all_to_all | solution.py:175
  124.1 0.7 shard_map.116
Async XLA Ops:
  0.6 51.6 %collective-permute-start.2 = (bf16[128,256]{1,0:T(8,128)(2,1)}, bf16[128,256]{1,0:T(8,128)(2,1)S(1)}, u32[]{:S(2)}, u32[]{:S(2)}) collective-permute-start(bf16[128,256]{1,0:T(8,128)(2,1)} %param.9), channel_id=1, source_target_pairs={{0,16},{8,24},{16,32},{24,40},{32,48},{40,56},{48,64},{56,72},{64,... | collective-permute-start | bytes 196616 | tf_op jit(solution)/shard_map/ppermute | solution.py:21
  7.3 44.9 %collective-permute-start.1 = (bf16[128,256]{1,0:T(8,128)(2,1)}, bf16[128,256]{1,0:T(8,128)(2,1)S(1)}, u32[]{:S(2)}, u32[]{:S(2)}) collective-permute-start(bf16[128,256]{1,0:T(8,128)(2,1)} %param.9), channel_id=1, source_target_pairs={{0,8},{8,16},{16,24},{24,32},{32,40},{40,48},{48,56},{56,64},{64,7... | collective-permute-start | bytes 196616 | tf_op jit(solution)/shard_map/ppermute | solution.py:21
  11.3 40.9 %collective-permute-start = (bf16[128,256]{1,0:T(8,128)(2,1)}, bf16[128,256]{1,0:T(8,128)(2,1)S(1)}, u32[]{:S(2)}, u32[]{:S(2)}) collective-permute-start(bf16[128,256]{1,0:T(8,128)(2,1)} %param.9), channel_id=1, source_target_pairs={{0,1016},{8,0},{16,8},{24,16},{32,24},{40,32},{48,40},{56,48},{64,... | collective-permute-start | bytes 196616 | tf_op jit(solution)/shard_map/ppermute | solution.py:21
  30.7 21.5 %collective-permute-start.3 = (bf16[128,256]{1,0:T(8,128)(2,1)}, bf16[128,256]{1,0:T(8,128)(2,1)S(1)}, u32[]{:S(2)}, u32[]{:S(2)}) collective-permute-start(bf16[128,256]{1,0:T(8,128)(2,1)} %param.9), channel_id=1, source_target_pairs={{0,1008},{8,1016},{16,0},{24,8},{32,16},{40,24},{48,32},{56,40},{6... | collective-permute-start | bytes 196616 | tf_op jit(solution)/shard_map/ppermute | solution.py:21
  52.2 0.7 copy-start.2
  52.9 0.7 copy-start.4
  53.6 20.3 %copy-start = (bf16[256,256]{1,0:T(8,128)(2,1)S(1)}, bf16[256,256]{1,0:T(8,128)(2,1)}, u32[]{:S(2)}) copy-start(bf16[256,256]{1,0:T(8,128)(2,1)} %weight_ref.1) | copy-start | bytes 393220
  53.6 20.3 %copy-start.1 = (bf16[128,256]{1,0:T(8,128)(2,1)S(1)}, bf16[128,256]{1,0:T(8,128)(2,1)}, u32[]{:S(2)}) copy-start(bf16[128,256]{1,0:T(8,128)(2,1)} %cotangent_ref.1) | copy-start | bytes 196612
  53.6 20.3 %copy-start.3 = (f32[256]{0:T(256)S(1)}, f32[256]{0:T(256)}, u32[]{:S(2)}) copy-start(f32[256]{0:T(256)} %param.11) | copy-start | bytes 3076
